TPU v7x, 512 devices: a whole 4x8x8 slice. The times are simulated.
512 devices in a mesh: tok: 8 (over z_hi, x), blk: 64 (over z_lo, y, core).
Axes of the slice: x: 4, y: 8, z: 8 (z_hi: 2, z_lo: 4; z = z_hi * 4 + z_lo), core: 2. Of those that a mesh axis runs over, the one named last changes fastest.
Arguments:
- grad_out: bfloat16 [8192, 8192], P('tok', 'blk'), may hold values from -6 to 6
- acts: bfloat16 [8192, 8192], P('tok', 'blk'), may hold values from -6 to 6
- stat_old: float32 [8, 64, 512, 512], P('tok', 'blk'), may hold values from -1 to 6, as said below
- root_old: float32 [8, 64, 512, 512], P('tok', 'blk'), may hold values from -1 to 2, as said below
- assign: int32 [64, 8], P('blk'), may hold values from 0 to 7, as said below
Outputs:
- roots: float32 [8, 64, 512, 512], P('tok', 'blk')
- precond: float32 [8, 64, 256, 512], P('tok', 'blk')
Inputs may be any that keep to these rules, and one draw needn't show every extreme that they name: `assign`: row j gives each of its 8 slots a job 2 b + s with b < 4 and s in 0, 1; every job once in a row; slots 2 m and 2 m + 1 hold the two sides of one block. `stat_old`: each slot's matrix is symmetric and positive definite. `root_old`: each slot's matrix is symmetric.
All inputs are finite; a program needn't handle non-finite values.
Results may differ from a plain program's by a relative error of at most 0.0003.
Values may be sent and summed in bfloat16 or wider, within the bound.
A program may use at most 64 MiB of HBM per device.

v0:
```python
import math

import jax
import jax.numpy as jnp
from jax import lax
from jax.sharding import Mesh
from jax.sharding import PartitionSpec as P

ITERS = 2
TOK = ("tok_0", "tok_1")


BETA = 0.9
DAMPING = 0.001


def swapped(block, axis, stride):
    count = lax.axis_size(axis)
    route = []
    for low in range(count):
        high = low | 1 << stride
        if high != low and high < count:
            route += [(low, high), (high, low)]
    return lax.ppermute(block, axis, route)


def sum_in_order(pieces, axes, sequence):
    inside = pieces.shape[1:]
    pieces = pieces.reshape(*(lax.axis_size(a) for a in axes), *inside)
    pieces = jnp.moveaxis(pieces, sequence, range(len(axes))).reshape(-1, *inside)
    for k in sequence:
        pieces = lax.psum_scatter(pieces, axes[k], scatter_dimension=0, tiled=True)
    return pieces[0]


def in_blocks(x, dim, devices):
    dims = x.shape
    pieces = x.reshape(*dims[:dim], devices, dims[dim] // devices, *dims[dim + 1 :])
    return jnp.moveaxis(pieces, dim, 0)


def scatter_axes(x, axes, sequence, dim):
    devices = lax.axis_size(axes)
    return sum_in_order(in_blocks(x, dim, devices), axes, sequence)


def product(lhs_matrix, rhs_matrix):
    return jnp.dot(
        lhs_matrix, rhs_matrix, precision=lax.Precision.HIGHEST, preferred_element_type=jnp.float32
    )


def newton_root(statistic, warm_root, square):
    identity = jnp.eye(square.shape[0], dtype=jnp.float32)
    factor = BETA * statistic + (1.0 - BETA) * square + DAMPING * identity
    root_square = product(warm_root, warm_root)
    coupled = product(product(root_square, root_square), factor)
    current = warm_root
    for iteration in range(ITERS):
        update = (5.0 * identity - coupled) * 0.25
        current = product(current, update)
        if iteration + 1 < ITERS:
            update_square = product(update, update)
            coupled = product(product(update_square, update_square), coupled)
    return current


def block_partials(rows_part, cols_part, group_blocks, block_size, scaling):
    shaped = cols_part.reshape(cols_part.shape[0], group_blocks, block_size)
    return (
        jnp.einsum("tr,tgc->grc", rows_part, shaped, preferred_element_type=jnp.float32) * scaling
    )


def join_pair(mine, theirs, column, bit):
    lower = column // (1 << bit) % 2 == 0
    return jnp.where(
        lower, jnp.concatenate([mine, theirs], axis=1), jnp.concatenate([theirs, mine], axis=1)
    )


def shards(grad_out, acts, stat_old, root_old, assign):
    token_groups = lax.axis_size(TOK)
    blk_count = lax.axis_size("blk")
    column = lax.axis_index("blk")
    position = lax.axis_index(TOK)
    block_size = stat_old.shape[-1]
    shard_rows = grad_out.shape[0]
    all_tokens = shard_rows * token_groups
    scaling = 1.0 / math.sqrt(all_tokens)
    strips = grad_out.shape[1] * blk_count // block_size
    strip_bits = strips.bit_length() - 1
    blk_bits = blk_count.bit_length() - 1
    group_blocks = token_groups // 2
    cols_part = acts
    for bit in range(strip_bits):
        other_cols = swapped(cols_part, "blk", bit)
        cols_part = join_pair(cols_part, other_cols, column, bit)
    rows_part = grad_out
    for bit in range(strip_bits, blk_bits):
        other_rows = swapped(rows_part, "blk", bit)
        rows_part = join_pair(rows_part, other_rows, column, bit)
    job_table = assign[0]
    job_index = job_table[position]
    side_bit = job_index % 2
    partial_value = block_partials(rows_part, cols_part, group_blocks, block_size, scaling)
    halves = partial_value.reshape(group_blocks * 2, block_size // 2, block_size)[job_table]
    own_half = scatter_axes(halves, TOK, (1, 0), 0)[0]
    other_half = swapped(own_half, TOK, 0)
    chosen = jnp.where(
        side_bit == 0,
        jnp.concatenate([own_half, other_half], axis=0),
        jnp.concatenate([other_half, own_half], axis=0),
    )
    oriented = jnp.where(side_bit == 0, chosen, chosen.T)
    square = product(oriented, oriented.T) / all_tokens
    own_root = newton_root(stat_old[0, 0], root_old[0, 0], square)
    other_root = swapped(own_root, TOK, 0)
    left_root = jnp.where(side_bit == 0, own_root, other_root)
    right_root = jnp.where(side_bit == 0, other_root, own_root)
    half_rows = lax.dynamic_slice_in_dim(
        left_root, side_bit * (block_size // 2), block_size // 2, 0
    )
    precond = product(product(half_rows, chosen), right_root)
    return (own_root[None, None], precond[None, None])


def solution(mesh):
    torus = Mesh(mesh.devices.reshape(2, 4, mesh.shape["blk"]), ("tok_0", "tok_1", "blk"))
    placed = (
        P(TOK, "blk"),
        P(TOK, "blk"),
        P(TOK, "blk", None, None),
        P(TOK, "blk", None, None),
        P("blk", None),
    )
    return jax.shard_map(
        shards,
        mesh=torus,
        in_specs=placed,
        out_specs=(P(TOK, "blk", None, None), P(TOK, "blk", None, None)),
        check_vma=False,
    )
```

profile of v0, /device:TPU:4, one launch (start us, length us, event | category | flops | bytes accessed | tf_op | source)
XLA Modules:
  0.0 375.5 jit_solution(3711299806003080079)
XLA Ops:
  7.2 2.1 collective-permute-start
  12.2 3.5 collective-permute-start.1
  15.7 12.3 %collective-permute-done.1 = bf16[1024,256]{1,0:T(8,128)(2,1)S(1)} collective-permute-done((bf16[1024,256]{1,0:T(8,128)(2,1)S(1)}, bf16[1024,256]{1,0:T(8,128)(2,1)S(1)}, u32[]{:S(2)}, u32[]{:S(2)}) %collective-permute-start.1) | collective-permute-done | bytes 524320 | tf_op jit(solution)/shard_map/ppermute | solution.py:24
  29.2 4.5 %collective-permute-start.2 = (bf16[1024,512]{1,0:T(8,128)(2,1)}, bf16[1024,512]{1,0:T(8,128)(2,1)S(1)}, u32[]{:S(2)}, u32[]{:S(2)}) collective-permute-start(bf16[1024,512]{1,0:T(8,128)(2,1)} %maximum_select_fusion.7), channel_id=1, source_target_pairs={{0,4},{4,0},{1,5},{5,1},{2,6},{6,2},{3,7},{7,3},{8,12},{12,8},{9,1... | collective-permute-start | bytes 3145736 | tf_op jit(solution)/shard_map/ppermute | solution.py:24
  33.8 45.3 %collective-permute-done.2 = bf16[1024,512]{1,0:T(8,128)(2,1)S(1)} collective-permute-done((bf16[1024,512]{1,0:T(8,128)(2,1)}, bf16[1024,512]{1,0:T(8,128)(2,1)S(1)}, u32[]{:S(2)}, u32[]{:S(2)}) %collective-permute-start.2) | collective-permute-done | bytes 1048608 | tf_op jit(solution)/shard_map/ppermute | solution.py:24
  79.1 3.7 maximum_select_fusion.3
  82.8 7.7 %collective-permute-start.3 = (bf16[1024,1024]{1,0:T(8,128)(2,1)}, bf16[1024,1024]{1,0:T(8,128)(2,1)}, u32[]{:S(2)}, u32[]{:S(2)}) collective-permute-start(bf16[1024,1024]{1,0:T(8,128)(2,1)} %maximum_select_fusion.3), channel_id=1, source_target_pairs={{0,8},{8,0},{1,9},{9,1},{2,10},{10,2},{3,11},{11,3},{4,12},{12,4},... | collective-permute-start | bytes 6291464 | tf_op jit(solution)/shard_map/ppermute | solution.py:24
  90.5 4.3 %collective-permute-start.4 = (bf16[1024,128]{1,0:T(8,128)(2,1)S(1)}, bf16[1024,128]{1,0:T(8,128)(2,1)}, u32[]{:S(2)}, u32[]{:S(2)}) collective-permute-start(bf16[1024,128]{1,0:T(8,128)(2,1)S(1)} %copy-done.4), channel_id=1, source_target_pairs={{0,16},{16,0},{1,17},{17,1},{2,18},{18,2},{3,19},{19,3},{4,20},{20... | collective-permute-start | bytes 786440 | tf_op jit(solution)/shard_map/ppermute | solution.py:24
  94.8 6.2 %collective-permute-done.4 = bf16[1024,128]{1,0:T(8,128)(2,1)} collective-permute-done((bf16[1024,128]{1,0:T(8,128)(2,1)S(1)}, bf16[1024,128]{1,0:T(8,128)(2,1)}, u32[]{:S(2)}, u32[]{:S(2)}) %collective-permute-start.4) | collective-permute-done | bytes 262176 | tf_op jit(solution)/shard_map/ppermute | solution.py:24
  101.0 2.0 maximum_select_fusion.11
  102.9 6.1 %collective-permute-start.5 = (bf16[1024,256]{1,0:T(8,128)(2,1)}, bf16[1024,256]{1,0:T(8,128)(2,1)}, u32[]{:S(2)}, u32[]{:S(2)}) collective-permute-start(bf16[1024,256]{1,0:T(8,128)(2,1)} %maximum_select_fusion.11), channel_id=1, source_target_pairs={{0,32},{32,0},{1,33},{33,1},{2,34},{34,2},{3,35},{35,3},{4,36},{36... | collective-permute-start | bytes 1572872 | tf_op jit(solution)/shard_map/ppermute | solution.py:24
  109.7 72.4 %collective-permute-done.3 = bf16[1024,1024]{1,0:T(8,128)(2,1)} collective-permute-done((bf16[1024,1024]{1,0:T(8,128)(2,1)}, bf16[1024,1024]{1,0:T(8,128)(2,1)}, u32[]{:S(2)}, u32[]{:S(2)}) %collective-permute-start.3) | collective-permute-done | bytes 2097184 | tf_op jit(solution)/shard_map/ppermute | solution.py:24
  183.9 6.4 %broadcast_multiply_fusion = f32[4,512,512]{1,2,0:T(8,128)} fusion(bf16[1024,2,512]{2,0,1:T(8,128)(2,1)S(1)} %bitcast.54, bf16[1024,2,512]{2,0,1:T(8,128)(2,1)S(1)} %maximum_select_fusion.2, pred[]{:T(512)S(6)} %eq.41, bf16[1024,256]{1,0:T(8,128)(2,1)} %collective-permute-done.5, bf16[1024,256]{1,0:T(8,128)(2,1)} %maximum_select_fusion.11, pred[]{:T(512)S(6)} %eq.45), kind=kOutput, calls=%fused_computation.12 | convolution fusion | flops 2159542272 | bytes 9437186 | tf_op jit(solution)/shard_map/tr,tgc->grc/dot_general | solution.py:71
  190.3 5.0 %gather_fusion = f32[8,256,512]{2,1,0:T(8,128)} fusion(f32[8,256,512]{2,1,0:T(8,128)} %bitcast.52, s32[1024]{0:T(1024)S(1)} %pad_clamp_fusion), kind=kCustom, calls=%fused_computation | custom fusion | bytes 8388640 | tf_op jit(solution)/shard_map/gather | solution.py:107
  195.2 5.2 %copy.10 = f32[2,4,1,256,512]{3,4,0,1,2:T(8,128)} copy(f32[2,4,1,256,512]{4,3,1,0,2:T(8,128)} %bitcast.48) | data formatting | bytes 8388608 | tf_op jit(solution)/shard_map/reshape;reshape | solution.py:29
  200.6 52.5 %reduce-scatter.3.cloned.1.call-done = f32[2,1,256,512]{2,3,1,0:T(8,128)} async-done(((f32[8,1,256,512]{2,3,1,0:T(8,128)}), f32[2,1,256,512]{2,3,1,0:T(8,128)}) %reduce-scatter.3.cloned.1.call-update) | async-done | bytes 1048592 | tf_op jit(solution)/shard_map/reduce_scatter | solution.py:32
  255.6 45.9 %reduce-scatter.5.cloned.1.call-done = f32[1,1,256,512]{2,3,1,0:T(8,128)} async-done(((f32[2,1,256,512]{2,3,1,0:T(8,128)}), f32[1,1,256,512]{2,3,1,0:T(8,128)}) %reduce-scatter.5.cloned.1.call-update) | async-done | bytes 524304 | tf_op jit(solution)/shard_map/reduce_scatter | solution.py:32
  301.5 3.2 collective-permute-start.6
  304.8 1.8 fusion.20
  306.6 1.8 fusion.47
  308.5 8.8 %collective-permute-done.6 = f32[256,512]{0,1:T(8,128)S(1)} collective-permute-done((f32[256,512]{0,1:T(8,128)}, f32[256,512]{0,1:T(8,128)S(1)}, u32[]{:S(2)}, u32[]{:S(2)}) %collective-permute-start.6) | collective-permute-done | bytes 524320 | tf_op jit(solution)/shard_map/ppermute | solution.py:24
  319.5 4.9 %fusion.8 = f32[512,512]{1,0:T(8,128)S(1)} fusion(f32[512,512]{1,0:T(8,128)} %copy.12, f32[1,1,512,512]{3,2,1,0:T(8,128)} %param.7, pred[]{:T(512)S(6)} %eq.40, f32[256,512]{0,1:T(8,128)} %copy-done.3, f32[256,512]{0,1:T(8,128)} %bitcast.56), kind=kOutput, calls=%fused_computation.17 | convolution fusion | flops 1613234176 | bytes 4194305 | tf_op jit(solution)/shard_map/dot_general | solution.py:48
  324.5 1.9 fusion.48
  326.3 1.9 fusion.24
  328.3 3.5 fusion.18
  331.8 2.1 fusion.49
  333.8 1.9 fusion.9
  335.7 1.8 fusion.50
  337.6 3.7 collective-permute-start.7
  341.3 22.8 %collective-permute-done.7 = f32[512,512]{1,0:T(8,128)S(1)} collective-permute-done((f32[512,512]{1,0:T(8,128)S(1)}, f32[512,512]{1,0:T(8,128)S(1)}, u32[]{:S(2)}, u32[]{:S(2)}) %collective-permute-start.7) | collective-permute-done | bytes 1048608 | tf_op jit(solution)/shard_map/ppermute | solution.py:24
  364.1 2.7 fusion.27
  366.8 1.9 convolution_bitcast_fusion
  (28 shorter events, 9.4 us)
Async XLA Ops:
  7.2 297.6 %copy-start = (f32[1,1,512,512]{3,2,1,0:T(8,128)S(1)}, f32[1,1,512,512]{3,2,1,0:T(8,128)}, u32[]{:S(2)}) copy-start(f32[1,1,512,512]{3,2,1,0:T(8,128)} %param.8) | copy-start | bytes 3145732
  7.2 245.9 %reduce-scatter.3.cloned.1.call-start = ((), (), s32[]{:S(2)}) async-start(), calls=%async_computation.2 | async-start | bytes 5242880 | tf_op jit(solution)/shard_map/reduce_scatter | solution.py:32
  7.2 3.8 %collective-permute-start = (bf16[1024,128]{1,0:T(8,128)(2,1)}, bf16[1024,128]{1,0:T(8,128)(2,1)S(1)}, u32[]{:S(2)}, u32[]{:S(2)}) collective-permute-start(bf16[1024,128]{1,0:T(8,128)(2,1)} %param.6), channel_id=1, source_target_pairs={{0,1},{1,0},{2,3},{3,2},{4,5},{5,4},{6,7},{7,6},{8,9},{9,8},{10,11... | collective-permute-start | bytes 786440 | tf_op jit(solution)/shard_map/ppermute | solution.py:24
  12.2 15.9 %collective-permute-start.1 = (bf16[1024,256]{1,0:T(8,128)(2,1)S(1)}, bf16[1024,256]{1,0:T(8,128)(2,1)S(1)}, u32[]{:S(2)}, u32[]{:S(2)}) collective-permute-start(bf16[1024,256]{1,0:T(8,128)(2,1)S(1)} %maximum_select_fusion.10), channel_id=1, source_target_pairs={{0,2},{2,0},{1,3},{3,1},{4,6},{6,4},{5,7},{7,5},{8,10},{10,8},{9,1... | collective-permute-start | bytes 1572872 | tf_op jit(solution)/shard_map/ppermute | solution.py:24
  29.2 49.8 %collective-permute-start.2 = (bf16[1024,512]{1,0:T(8,128)(2,1)}, bf16[1024,512]{1,0:T(8,128)(2,1)S(1)}, u32[]{:S(2)}, u32[]{:S(2)}) collective-permute-start(bf16[1024,512]{1,0:T(8,128)(2,1)} %maximum_select_fusion.7), channel_id=1, source_target_pairs={{0,4},{4,0},{1,5},{5,1},{2,6},{6,2},{3,7},{7,3},{8,12},{12,8},{9,1... | collective-permute-start | bytes 3145736 | tf_op jit(solution)/shard_map/ppermute | solution.py:24
  33.8 56.7 %copy-start.4 = (bf16[1024,128]{1,0:T(8,128)(2,1)S(1)}, bf16[1024,128]{1,0:T(8,128)(2,1)}, u32[]{:S(2)}) copy-start(bf16[1024,128]{1,0:T(8,128)(2,1)} %param.5) | copy-start | bytes 786436
  33.8 75.2 %copy-start.5 = (s32[1,8]{1,0:T(1,128)S(1)}, s32[1,8]{1,0:T(1,128)}, u32[]{:S(2)}) copy-start(s32[1,8]{1,0:T(1,128)} %param.9) | copy-start | bytes 100
  82.8 99.4 %collective-permute-start.3 = (bf16[1024,1024]{1,0:T(8,128)(2,1)}, bf16[1024,1024]{1,0:T(8,128)(2,1)}, u32[]{:S(2)}, u32[]{:S(2)}) collective-permute-start(bf16[1024,1024]{1,0:T(8,128)(2,1)} %maximum_select_fusion.3), channel_id=1, source_target_pairs={{0,8},{8,0},{1,9},{9,1},{2,10},{10,2},{3,11},{11,3},{4,12},{12,4},... | collective-permute-start | bytes 6291464 | tf_op jit(solution)/shard_map/ppermute | solution.py:24
  90.5 10.5 %collective-permute-start.4 = (bf16[1024,128]{1,0:T(8,128)(2,1)S(1)}, bf16[1024,128]{1,0:T(8,128)(2,1)}, u32[]{:S(2)}, u32[]{:S(2)}) collective-permute-start(bf16[1024,128]{1,0:T(8,128)(2,1)S(1)} %copy-done.4), channel_id=1, source_target_pairs={{0,16},{16,0},{1,17},{17,1},{2,18},{18,2},{3,19},{19,3},{4,20},{20... | collective-permute-start | bytes 786440 | tf_op jit(solution)/shard_map/ppermute | solution.py:24
  102.9 80.9 %collective-permute-start.5 = (bf16[1024,256]{1,0:T(8,128)(2,1)}, bf16[1024,256]{1,0:T(8,128)(2,1)}, u32[]{:S(2)}, u32[]{:S(2)}) collective-permute-start(bf16[1024,256]{1,0:T(8,128)(2,1)} %maximum_select_fusion.11), channel_id=1, source_target_pairs={{0,32},{32,0},{1,33},{33,1},{2,34},{34,2},{3,35},{35,3},{4,36},{36... | collective-permute-start | bytes 1572872 | tf_op jit(solution)/shard_map/ppermute | solution.py:24
  200.5 101.0 %reduce-scatter.5.cloned.1.call-start = ((), (), s32[]{:S(2)}) async-start(), calls=%async_computation.3 | async-start | bytes 1572864 | tf_op jit(solution)/shard_map/reduce_scatter | solution.py:32
  301.5 15.8 %collective-permute-start.6 = (f32[256,512]{0,1:T(8,128)}, f32[256,512]{0,1:T(8,128)S(1)}, u32[]{:S(2)}, u32[]{:S(2)}) collective-permute-start(f32[256,512]{0,1:T(8,128)} %bitcast.55), channel_id=1, source_target_pairs={{0,64},{64,0},{128,192},{192,128},{256,320},{320,256},{384,448},{4... | collective-permute-start | bytes 1572872 | tf_op jit(solution)/shard_map/ppermute | solution.py:24
  306.6 11.4 %copy-start.2 = (f32[1,1,256,512]{2,3,1,0:T(8,128)S(1)}, f32[1,1,256,512]{2,3,1,0:T(8,128)}, u32[]{:S(2)}) copy-start(f32[1,1,256,512]{2,3,1,0:T(8,128)} %reduce-scatter.5.cloned.1.call-done) | copy-start | bytes 1572868
  317.3 0.8 copy-start.3
  337.5 31.1 %copy-start.1 = (f32[512,512]{1,0:T(8,128)}, f32[512,512]{1,0:T(8,128)S(1)}, u32[]{:S(2)}) copy-start(f32[512,512]{1,0:T(8,128)S(1)} %fusion.50) | copy-start | bytes 3145732
  337.6 26.5 %collective-permute-start.7 = (f32[512,512]{1,0:T(8,128)S(1)}, f32[512,512]{1,0:T(8,128)S(1)}, u32[]{:S(2)}, u32[]{:S(2)}) collective-permute-start(f32[512,512]{1,0:T(8,128)S(1)} %fusion.50), channel_id=1, source_target_pairs={{0,64},{64,0},{128,192},{192,128},{256,320},{320,256},{384,448},{4... | collective-permute-start | bytes 3145736 | tf_op jit(solution)/shard_map/ppermute | solution.py:24
Sparse Core Ops, SparseCore 0:
  200.6 52.3 reduce-scatter.2
  256.1 45.4 reduce-scatter.4
where the time goes:
time: 376 us
  waiting for transfers between devices  268 us (71%)
  starting transfers between devices  35.1 us (9%)
  matrix products  32.6 us (9%)
  between operations  16.4 us (4%)
  local copies, waits for them, and re-layouts  14.7 us (4%)
  other arithmetic  8.78 us (2%)
    ppermute x8, waiting for transfers between devices, swapped(): return lax.ppermute(block, axis, route)  169 us
    reduce_scatter x2, waiting for transfers between devices, sum_in_order(): pieces = lax.psum_scatter(pieces, axes[k], scatter_dimension=0, tiled=True)  98.4 us
    ppermute x8, starting transfers between devices, swapped(): return lax.ppermute(block, axis, route)  35 us
    dot_general x11, matrix products, product(): jnp.dot(lhs_matrix, rhs_matrix, precision=lax.Precision.HIGHEST, preferre...  26.2 us
    select_n x6, other arithmetic, join_pair(): jnp.where(lower, jnp.concatenate([mine, theirs], axis=1), jnp.concatenate...  8.61 us
  transfers between devices with their start and end apart: 10, of which 9 were waited for; matrix products, arithmetic and copies ran while one was open for 2% of the time, Pallas kernels for 0%

commit v1 on v0

v1 whole, which is shorter than its diff:
```python
import math

import jax
import jax.numpy as jnp
from jax import lax
from jax.experimental import pallas as pl
from jax.experimental.pallas import tpu as pltpu
from jax.sharding import PartitionSpec as P

BETA = 0.9
DAMPING = 0.001
MESH = pl.DeviceIdType.MESH
BF = jnp.bfloat16
F32 = jnp.float32
X, Z_HI, Y, Z_LO, CORES = 4, 2, 8, 4, 2
BS = 512
HALF = 256
UNIT = 128
TOK = 1024
TH = 512
SHARD = 128
STEPS = 32767.0


def split(v):
    hi = v.astype(BF)
    lo = (v - hi.astype(F32)).astype(BF)
    return hi, lo


def dot(a, b):
    return jnp.dot(a, b, preferred_element_type=F32)


def dot_nt(a, b):
    return lax.dot_general(a, b, (((1,), (1,)), ((), ())), preferred_element_type=F32)


def mm3(a, b, d=dot):
    return d(a[0], b[0]) + (d(a[0], b[1]) + d(a[1], b[0]))


def encode(v):
    top = jnp.maximum(jnp.max(jnp.abs(v), axis=0, keepdims=True), 1e-30)
    code = jnp.round(v * (STEPS / top)).astype(jnp.int32).astype(jnp.int16)
    return code, top * (1.0 / STEPS)


def decode(code, step):
    return code.astype(jnp.int32).astype(F32) * step


def kernel(
    assign, grad, acts, stat_hbm, root_hbm, roots_out, precond_out,
    cols, rows, stat, root, hold, grad_full, ori, r2, r4, mat, upd, cur, upd2, tmp, mine, other, pre,
    xcs, xcr, xss, xsr, zcs, zcr, zss, zsr, acs, acr, ass_, asr, rcs, rcr, rss, rsr,
    loc_sem, ys, yr, sibs, sibr, ws, wr, xs, xr, zs, zr, as_, ar, rs, rr, out_sem,
):
    t = lax.axis_index("tok")
    j = lax.axis_index("blk")
    x = lax.rem(t, X)
    h = lax.div(t, X)
    core = lax.rem(j, CORES)
    y = lax.rem(lax.div(j, CORES), Y)
    w = lax.div(j, CORES * Y)

    def y_dev(d):
        return (t, w * (CORES * Y) + lax.rem(y + d + Y, Y) * CORES + core)

    def w_dev(d):
        return (t, lax.rem(w + d + Z_LO, Z_LO) * (CORES * Y) + y * CORES + core)

    def x_dev(d):
        return (h * X + lax.rem(x + d + X, X), j)

    sibling = (t, j + 1 - 2 * core)
    z_dev = ((1 - h) * X + x, j)
    pair_dev = (t + 1 - 2 * lax.rem(x, 2), j)

    partners = [sibling, z_dev] + [y_dev(d) for d in (1, -1)] + [w_dev(d) for d in (1, 2, 3)] + [x_dev(d) for d in (1, -1)]

    stat_in = pltpu.make_async_copy(stat_hbm, stat, loc_sem.at[0])
    root_in = pltpu.make_async_copy(root_hbm, root, loc_sem.at[1])
    root_in.start()
    stat_in.start()

    barrier = pltpu.get_barrier_semaphore()
    for dev in partners:
        pl.semaphore_signal(barrier, inc=1, device_id=dev, device_id_type=MESH)
    pl.semaphore_wait(barrier, len(partners))

    sends = []

    def remote(src, dst, ssem, rsem, dev):
        return pltpu.make_async_remote_copy(
            src_ref=src, dst_ref=dst, send_sem=ssem, recv_sem=rsem, device_id=dev, device_id_type=MESH
        )

    def start(src, dst, ssem, rsem, dev):
        copy = remote(src, dst, ssem, rsem, dev)
        copy.start()
        sends.append(copy)

    def landed(dst, ssem, rsem, dev):
        remote(dst, dst, ssem, rsem, dev).wait_recv()

    def shard(d, c):
        return lax.rem(y + d + Y, Y) * CORES + c

    def part(k):
        return pl.ds(k * TH, TH)

    own = shard(0, core)
    for k in range(2):
        for side, step in ((0, 1), (1, -1)):
            start(acts.at[part(k)], cols.at[own, part(k)], ys.at[side, 0, k], yr.at[side, 0, k], y_dev(step))
    for k in range(2):
        start(acts.at[part(k)], cols.at[own, part(k)], sibs.at[14 + k], sibr.at[14 + k], sibling)
    own_in = pltpu.make_async_copy(acts, cols.at[own], loc_sem.at[2])
    own_in.start()
    rows[w] = grad[...].T
    for d in (1, 2, 3):
        start(rows.at[w], rows.at[w], ws.at[d - 1], wr.at[d - 1], w_dev(d))

    root_in.wait()
    x0 = split(root[...])
    mine[0] = x0[0]
    mine[1] = x0[1]
    v = split(mm3(x0, x0))
    r2[0] = v[0]
    r2[1] = v[1]

    arrivals = []
    number = 0
    for d in (1, 2, 3, 4):
        for k in range(2):
            for side, step in ((0, 1), (1, -1)):
                if d == 4 and k != side:
                    continue
                region = cols.at[shard(-step * d, core), part(k)]
                landed(region, ys.at[side, d - 1, k], yr.at[side, d - 1, k], y_dev(-step))
                if d < 3 or (d == 3 and k == side):
                    start(region, region, ys.at[side, d, k], yr.at[side, d, k], y_dev(step))
                start(region, region, sibs.at[number], sibr.at[number], sibling)
                arrivals.append((shard(-step * d, 1 - core), k, number))
                number += 1

    for k in range(2):
        arrivals.append((shard(0, 1 - core), k, 14 + k))
    for index, k, n in arrivals:
        landed(cols.at[index, part(k)], sibs.at[n], sibr.at[n], sibling)
    own_in.wait()
    for d in (1, 2, 3):
        region = rows.at[lax.rem(w - d + Z_LO, Z_LO)]
        landed(region, ws.at[d - 1], wr.at[d - 1], w_dev(-d))

    scaling = 1.0 / math.sqrt(TOK * X * Z_HI)

    def piece(far, d):
        to_h = 1 - h if far == 0 else h
        to_x = lax.rem(x + d + X, X)
        pair = to_h * 2 + lax.div(to_x, 2)
        block = lax.div(assign[0, 2 * pair], 2)
        left = rows[pl.ds(2 * lax.rem(to_x, 2), 2)].reshape(HALF, TOK)
        right = jnp.concatenate([cols[4 * block + i] for i in range(4)], axis=1)
        return dot(left, right) * scaling

    def x_send(side, far, kind, value):
        code, step = encode(value)
        xcs[side, far, kind] = code
        xss[side, far, kind] = step
        dev = x_dev(1 if side == 0 else -1)
        start(xcs.at[side, far, kind], xcr.at[side, far, kind], xs.at[0, side, far, kind], xr.at[0, side, far, kind], dev)
        start(xss.at[side, far, kind], xsr.at[side, far, kind], xs.at[1, side, far, kind], xr.at[1, side, far, kind], dev)

    def x_recv(side, far, kind):
        dev = x_dev(-1 if side == 0 else 1)
        landed(xcr.at[side, far, kind], xs.at[0, side, far, kind], xr.at[0, side, far, kind], dev)
        landed(xsr.at[side, far, kind], xs.at[1, side, far, kind], xr.at[1, side, far, kind], dev)
        return decode(xcr[side, far, kind], xsr[side, far, kind])

    def first(far):
        v = piece(far, 2)
        x_send(0, far, 0, v[:UNIT])
        x_send(1, far, 0, v[UNIT:])

    def second(far):
        v = piece(far, 1)
        x_send(0, far, 1, v[UNIT:])
        hold[far, 0] = v[:UNIT]
        v = piece(far, -1)
        x_send(1, far, 1, v[:UNIT])
        hold[far, 1] = v[UNIT:]

    def third(far):
        x_send(0, far, 2, hold[far, 0] + x_recv(0, far, 0))
        x_send(1, far, 2, hold[far, 1] + x_recv(1, far, 0))

    def keep(far):
        v = piece(far, 0)
        hold[far, 2] = v[:UNIT]
        hold[far, 3] = v[UNIT:]

    def summed(far, u):
        if u == 0:
            return hold[far, 2] + x_recv(0, far, 2) + x_recv(1, far, 1)
        return hold[far, 3] + x_recv(0, far, 1) + x_recv(1, far, 2)

    first(0)
    second(0)
    first(1)
    third(0)
    second(1)
    keep(0)
    third(1)
    for u in range(2):
        code, step = encode(summed(0, u))
        zcs[u] = code
        zss[u] = step
        start(zcs.at[u], zcr.at[u], zs.at[0, u], zr.at[0, u], z_dev)
        start(zss.at[u], zsr.at[u], zs.at[1, u], zr.at[1, u], z_dev)
    keep(1)

    v = (r2[0], r2[1])
    v = split(mm3(v, v))
    r4[0] = v[0]
    r4[1] = v[1]

    low = 2 * lax.rem(x, 2)
    for u in range(2):
        v = summed(1, u)
        landed(zcr.at[u], zs.at[0, u], zr.at[0, u], z_dev)
        landed(zsr.at[u], zs.at[1, u], zr.at[1, u], z_dev)
        v = v + decode(zcr[u], zsr[u])
        code, step = encode(v)
        acs[u] = code
        ass_[u] = step
        start(acs.at[u], acr.at[u], as_.at[0, u], ar.at[0, u], pair_dev)
        start(ass_.at[u], asr.at[u], as_.at[1, u], ar.at[1, u], pair_dev)
        grad_full[low + u] = v
    for u in range(2):
        landed(acr.at[u], as_.at[0, u], ar.at[0, u], pair_dev)
        landed(asr.at[u], as_.at[1, u], ar.at[1, u], pair_dev)
        grad_full[2 - low + u] = decode(acr[u], asr[u])

    side_bit = lax.rem(assign[0, t], 2)
    g = grad_full[...].reshape(BS, BS)
    v = split(jnp.where(side_bit == 0, g, g.T))
    ori[0] = v[0]
    ori[1] = v[1]
    stat_in.wait()

    def eye(low_row, count):
        r = lax.broadcasted_iota(jnp.int32, (count, BS), 0) + low_row
        c = lax.broadcasted_iota(jnp.int32, (count, BS), 1)
        return r == c

    def both(ref):
        return ref[0], ref[1]

    def chunk(ref, q):
        return ref[0, pl.ds(q * HALF, HALF)], ref[1, pl.ds(q * HALF, HALF)]

    def put(ref, q, value):
        value = split(value)
        ref[0, pl.ds(q * HALF, HALF)] = value[0]
        ref[1, pl.ds(q * HALF, HALF)] = value[1]

    def update(value, q):
        return (jnp.where(eye(q * HALF, HALF), 5.0, 0.0) - value) * 0.25

    tokens = float(TOK * X * Z_HI)
    for q in range(2):
        square = mm3(chunk(ori, q), both(ori), dot_nt) * (1.0 / tokens)
        damp = jnp.where(eye(q * HALF, HALF), DAMPING, 0.0)
        put(tmp, q, BETA * stat[pl.ds(q * HALF, HALF)] + (1.0 - BETA) * square + damp)
    for q in range(2):
        v = mm3(chunk(r4, q), both(tmp))
        put(mat, q, v)
        put(upd, q, update(v, q))
    for q in range(2):
        put(upd2, q, mm3(chunk(upd, q), both(upd)))
    for q in range(2):
        put(cur, q, mm3(chunk(mine, q), both(upd)))
    for q in range(2):
        put(tmp, q, mm3(chunk(upd2, q), both(upd2)))
    for q in range(2):
        put(upd, q, update(mm3(chunk(tmp, q), both(mat)), q))
    outs = []
    for q in (1, 0):
        v = mm3(chunk(cur, q), both(upd))
        for i in range(2):
            u = 2 * q + i
            value = v[i * UNIT:(i + 1) * UNIT]
            on = eye(u * UNIT, UNIT)
            code, step = encode(jnp.where(on, 0.0, value))
            rcs[u] = code
            rss[u, 0:1] = step
            rss[u, 1:2] = jnp.sum(jnp.where(on, value, 0.0), axis=0, keepdims=True)
            start(rcs.at[u], rcr.at[u], rs.at[0, u], rr.at[0, u], pair_dev)
            start(rss.at[u], rsr.at[u], rs.at[1, u], rr.at[1, u], pair_dev)
        root[pl.ds(q * HALF, HALF)] = v
        copy = pltpu.make_async_copy(root.at[pl.ds(q * HALF, HALF)], roots_out.at[pl.ds(q * HALF, HALF)], out_sem.at[q])
        copy.start()
        outs.append(copy)
        put(mine, q, v)
    v = split(grad_full[...].reshape(BS, BS))
    ori[0] = v[0]
    ori[1] = v[1]

    def arrived(u):
        landed(rcr.at[u], rs.at[0, u], rr.at[0, u], pair_dev)
        landed(rsr.at[u], rs.at[1, u], rr.at[1, u], pair_dev)
        value = decode(rcr[u], rsr[u, 0:1]) + jnp.where(eye(u * UNIT, UNIT), rsr[u, 1:2], 0.0)
        value = split(value)
        other[0, pl.ds(u * UNIT, UNIT)] = value[0]
        other[1, pl.ds(u * UNIT, UNIT)] = value[1]

    arrived(2)
    arrived(3)
    half = tuple(
        jnp.where(side_bit == 0, a, b) for a, b in zip(chunk(mine, 0), chunk(other, 1))
    )
    v = split(mm3(half, both(ori)))
    pre[0] = v[0]
    pre[1] = v[1]
    arrived(0)
    arrived(1)
    right = tuple(jnp.where(side_bit == 0, b, a) for a, b in zip(both(mine), both(other)))
    final = mm3(both(pre), right)
    stat[pl.ds(0, HALF)] = final
    copy = pltpu.make_async_copy(stat.at[pl.ds(0, HALF)], precond_out, out_sem.at[2])
    copy.start()
    outs.append(copy)
    for copy in sends:
        copy.wait_send()
    for copy in outs:
        copy.wait()


def shards(grad_out, acts, stat_old, root_old, assign):
    def wide(*shape):
        return pltpu.VMEM((*shape, UNIT, BS), jnp.int16)

    def steps(*shape):
        return pltpu.VMEM((*shape, 1, BS), F32)

    def pair_of(rows_):
        return pltpu.VMEM((2, rows_, BS), BF)

    dma = pltpu.SemaphoreType.DMA
    anywhere = pl.BlockSpec(memory_space=pl.ANY)
    vmem = pl.BlockSpec(memory_space=pltpu.VMEM)
    roots, precond = pl.pallas_call(
        kernel,
        out_shape=(
            jax.ShapeDtypeStruct((BS, BS), F32),
            jax.ShapeDtypeStruct((HALF, BS), F32),
        ),
        in_specs=[pl.BlockSpec(memory_space=pltpu.SMEM), vmem, vmem, anywhere, anywhere],
        out_specs=(anywhere, anywhere),
        scratch_shapes=[
            pltpu.VMEM((CORES * Y, TOK, SHARD), BF),
            pltpu.VMEM((Z_LO, SHARD, TOK), BF),
            pltpu.VMEM((BS, BS), F32),
            pltpu.VMEM((BS, BS), F32),
            pltpu.VMEM((2, 4, UNIT, BS), F32),
            pltpu.VMEM((4, UNIT, BS), F32),
            *[pair_of(BS) for _ in range(10)],
            pair_of(HALF),
            wide(2, 2, 3), wide(2, 2, 3), steps(2, 2, 3), steps(2, 2, 3),
            wide(2), wide(2), steps(2), steps(2),
            wide(2), wide(2), steps(2), steps(2),
            wide(4), wide(4),
            pltpu.VMEM((4, 2, BS), F32), pltpu.VMEM((4, 2, BS), F32),
            dma((3,)),
            dma((2, 4, 2)), dma((2, 4, 2)),
            dma((16,)), dma((16,)),
            dma((3,)), dma((3,)),
            dma((2, 2, 2, 3)), dma((2, 2, 2, 3)),
            dma((2, 2)), dma((2, 2)),
            dma((2, 2)), dma((2, 2)),
            dma((2, 4)), dma((2, 4)),
            dma((3,)),
        ],
        compiler_params=pltpu.CompilerParams(
            collective_id=0, has_side_effects=True, vmem_limit_bytes=56 * 2**20
        ),
    )(assign, grad_out, acts, stat_old[0, 0], root_old[0, 0])
    return roots[None, None], precond[None, None]


def solution(mesh):
    placed = (
        P("tok", "blk"),
        P("tok", "blk"),
        P("tok", "blk", None, None),
        P("tok", "blk", None, None),
        P("blk", None),
    )
    return jax.shard_map(
        shards,
        mesh=mesh,
        in_specs=placed,
        out_specs=(P("tok", "blk", None, None), P("tok", "blk", None, None)),
        check_vma=False,
    )
```

time: 376 us -> 96.6 us (0.26)
  the two profiles are of different devices: /device:TPU:4 before, /device:TPU:152 now
where the time goes in v1:
time: 96.6 us; the launch traced here: 96.4 us
  Pallas kernels  92.6 us (96%)
  local copies, waits for them, and re-layouts  3.12 us (3%)
    pallas_call x1, Pallas kernels, shards(): pl.pallas_call(kernel, out_shape=(jax.ShapeDtypeStruct((BS, BS), F32), ja...  92.6 us
    unnamed x4, local copies, waits for them, and re-layouts  3.12 us

profile of v1, /device:TPU:152, one launch (start us, length us, event | category | flops | bytes accessed | tf_op | source)
XLA Modules:
  0.0 96.4 jit_solution(850889961853992928)
XLA Ops:
  0.6 92.6 %shard_map.68 = (f32[512,512]{1,0:T(8,128)}, f32[256,512]{1,0:T(8,128)}) custom-call(s32[1,8]{1,0:T(1,128)} %assign.1, bf16[1024,128]{1,0:T(8,128)(2,1)} %grad.1, bf16[1024,128]{1,0:T(8,128)(2,1)} %acts.1, f32[512,512]{1,0:T(8,128)} %bitcast.4, f32[512,512]{1,0:T(8,128)} %bitcast.5), custom_call_target="tpu_custom_call" | custom-call | tf_op jit(solution)/shard_map/pallas_call | solution.py:354
  93.3 0.0 copy-start
  93.3 2.3 %copy.9 = f32[1,1,512,512]{3,2,1,0:T(8,128)} copy(f32[1,1,512,512]{3,2,1,0:T(8,128)} %bitcast.6) | data formatting | bytes 2097152
  95.6 0.0 copy-done
  95.6 0.8 copy.10
Async XLA Ops:
  93.3 2.3 %copy-start = (f32[256,512]{1,0:T(8,128)S(1)}, f32[256,512]{1,0:T(8,128)}, u32[]{:S(2)}) copy-start(f32[256,512]{1,0:T(8,128)} %get-tuple-element.5) | copy-start | bytes 1572868

commit v2 on v1

v2 whole, which is shorter than its diff:
```python
import math

import jax
import jax.numpy as jnp
from jax import lax
from jax.experimental import pallas as pl
from jax.experimental.pallas import tpu as pltpu
from jax.sharding import PartitionSpec as P

BETA = 0.9
DAMPING = 0.001
MESH = pl.DeviceIdType.MESH
BF = jnp.bfloat16
F32 = jnp.float32
X, Z_HI, Y, Z_LO, CORES = 4, 2, 8, 4, 2
BS = 512
HALF = 256
UNIT = 128
TOK = 1024
QT = 256
SUB = 32
OFFSETS = (0, 1, -1, 2, -2, 3, -3, 4)
TURNS = (2, 1, -1, 0)
RIGHTWARD = (0, 1, 3, 5)
STRAIGHT = 7
SHARD = 128
STEPS = 32767.0


def split(v):
    hi = v.astype(BF)
    lo = (v - hi.astype(F32)).astype(BF)
    return hi, lo


def dot(a, b):
    return jnp.dot(a, b, preferred_element_type=F32)


def dot_nt(a, b):
    return lax.dot_general(a, b, (((1,), (1,)), ((), ())), preferred_element_type=F32)


def mm3(a, b, d=dot):
    return d(a[0], b[0]) + (d(a[0], b[1]) + d(a[1], b[0]))


def encode(v):
    top = jnp.maximum(jnp.max(jnp.abs(v), axis=0, keepdims=True), 1e-30)
    code = jnp.round(v * (STEPS / top)).astype(jnp.int32).astype(jnp.int16)
    return code, top * (1.0 / STEPS)


def decode(code, step):
    return code.astype(jnp.int32).astype(F32) * step


def kernel(
    assign, grad, acts, stat_hbm, root_hbm, roots_out, precond_out,
    cols, rows, stat, root, hold, grad_full, ori, r2, r4, mat, upd, cur, upd2, tmp, mine, other, pre,
    xcs, xcr, xss, xsr, zcs, zcr, zss, zsr, acs, acr, ass_, asr, rcs, rcr, rss, rsr,
    loc_sem, ys, yr, sibs, sibr, ws, wr, xs, xr, zs, zr, as_, ar, rs, rr,
):
    t = lax.axis_index("tok")
    j = lax.axis_index("blk")
    x = lax.rem(t, X)
    h = lax.div(t, X)
    core = lax.rem(j, CORES)
    y = lax.rem(lax.div(j, CORES), Y)
    w = lax.div(j, CORES * Y)

    def y_dev(d):
        return (t, w * (CORES * Y) + lax.rem(y + d + Y, Y) * CORES + core)

    def w_dev(d):
        return (t, lax.rem(w + d + Z_LO, Z_LO) * (CORES * Y) + y * CORES + core)

    def x_dev(d):
        return (h * X + lax.rem(x + d + X, X), j)

    sibling = (t, j + 1 - 2 * core)
    z_dev = ((1 - h) * X + x, j)
    pair_dev = (t + 1 - 2 * lax.rem(x, 2), j)

    partners = [sibling, z_dev] + [y_dev(d) for d in (1, -1)]
    partners += [dev(d) for dev in (w_dev, x_dev) for d in (1, 2, 3)]

    stat_in = pltpu.make_async_copy(stat_hbm, stat, loc_sem.at[0])
    root_in = pltpu.make_async_copy(root_hbm, root, loc_sem.at[1])
    root_in.start()
    stat_in.start()

    barrier = pltpu.get_barrier_semaphore()
    for dev in partners:
        pl.semaphore_signal(barrier, inc=1, device_id=dev, device_id_type=MESH)
    pl.semaphore_wait(barrier, len(partners))

    sends = []

    def remote(src, dst, ssem, rsem, dev):
        return pltpu.make_async_remote_copy(
            src_ref=src, dst_ref=dst, send_sem=ssem, recv_sem=rsem, device_id=dev, device_id_type=MESH
        )

    def start(src, dst, ssem, rsem, dev):
        copy = remote(src, dst, ssem, rsem, dev)
        copy.start()
        sends.append(copy)

    def landed(dst, ssem, rsem, dev):
        remote(dst, dst, ssem, rsem, dev).wait_recv()

    def at_y(d):
        return lax.rem(y + d + Y, Y)

    SIDES = ((0, 1), (1, -1))

    def part(q):
        return pl.ds(q * QT, QT)

    def ring(d):
        return [((n + 2 * side) % 4, side, step) for n in range(4 if d < 4 else 2) for side, step in SIDES]

    def number(d, q, side):
        return 24 + q if d == 4 else ((d - 1) * 4 + q) * 2 + side

    def y_step(d, parts):
        for q, side, step in ring(d):
            if (q + 2 * side) % 4 not in parts:
                continue
            region = cols.at[at_y(-step * d) * CORES + core, part(q)]
            landed(region, ys.at[side, d - 1, q], yr.at[side, d - 1, q], y_dev(-step))
            if d < 3 or (d == 3 and q // 2 == side):
                start(region, region, ys.at[side, d, q], yr.at[side, d, q], y_dev(step))
            n = number(d, q, side)
            start(region, region, sibs.at[n], sibr.at[n], sibling)

    def y_ready(d):
        if d == 0:
            own_in.wait()
            landed(cols.at[y * CORES + 1 - core], sibs.at[28], sibr.at[28], sibling)
            return
        for q, side, step in ring(d):
            n = number(d, q, side)
            landed(cols.at[at_y(-step * d) * CORES + 1 - core, part(q)], sibs.at[n], sibr.at[n], sibling)

    def quarter(e):
        return lax.rem(x + TURNS[e] + X, X)

    def rows_ready(e):
        for d in (2, 3, 1):
            unit = rows.at[quarter(e), lax.rem(w - d + Z_LO, Z_LO)]
            landed(unit, ws.at[e, d - 1], wr.at[e, d - 1], w_dev(-d))

    for q, side, step in ring(0):
        start(acts.at[part(q)], cols.at[y * CORES + core, part(q)], ys.at[side, 0, q], yr.at[side, 0, q], y_dev(step))
    start(acts, cols.at[y * CORES + core], sibs.at[28], sibr.at[28], sibling)
    own_in = pltpu.make_async_copy(acts, cols.at[y * CORES + core], loc_sem.at[2])
    own_in.start()
    v = grad[...].T
    for q in range(4):
        rows[q, w] = v[q * SUB:(q + 1) * SUB]

    def rows_send(e):
        unit = rows.at[quarter(e), w]
        for d in (2, 3, 1):
            start(unit, unit, ws.at[e, d - 1], wr.at[e, d - 1], w_dev(d))

    rows_send(0)
    root_in.wait()
    x0 = split(root[...])
    mine[0] = x0[0]
    mine[1] = x0[1]
    v = split(mm3(x0, x0))
    r2[0] = v[0]
    r2[1] = v[1]
    v = split(mm3(v, v))
    r4[0] = v[0]
    r4[1] = v[1]

    scaling = 1.0 / math.sqrt(TOK * X * Z_HI)

    def piece(e, g):
        left = rows[quarter(e)].reshape(UNIT, TOK)
        at = at_y(OFFSETS[g]) * CORES
        right = jnp.concatenate([cols[at], cols[at + 1]], axis=1)
        return dot(left, right) * scaling

    RIGHT, LEFT, FAR = 0, 1, 2

    def heading(slot, g):
        if slot == FAR:
            return 2 if g == STRAIGHT else (1 if g in RIGHTWARD else -1)
        return 1 if slot == RIGHT else -1

    def x_send(slot, g, value):
        code, step = encode(value)
        xcs[slot, g] = code
        xss[slot, g] = step
        dev = x_dev(heading(slot, g))
        start(xcs.at[slot, g], xcr.at[slot, g], xs.at[0, slot, g], xr.at[0, slot, g], dev)
        start(xss.at[slot, g], xsr.at[slot, g], xs.at[1, slot, g], xr.at[1, slot, g], dev)

    def x_take(slot, g):
        dev = x_dev(-heading(slot, g))
        landed(xcr.at[slot, g], xs.at[0, slot, g], xr.at[0, slot, g], dev)
        landed(xsr.at[slot, g], xs.at[1, slot, g], xr.at[1, slot, g], dev)
        return decode(xcr[slot, g], xsr[slot, g])

    def far(*gs):
        for g in gs:
            x_send(FAR, g, piece(0, g))

    def raw(slot, *gs):
        for g in gs:
            x_send(slot, g, piece(slot + 1, g))

    def add(slot, *gs):
        for g in gs:
            x_send(slot, g, piece(slot + 1, g) + x_take(FAR, g))

    y_step(1, (0, 1))
    rows_send(1)
    y_step(1, (2, 3))
    y_ready(0)
    y_ready(1)
    rows_ready(0)
    far(0, 2, 1)
    y_step(2, (0, 1))
    rows_send(2)
    y_step(2, (2, 3))
    y_ready(2)
    far(3, 4)
    rows_ready(1)
    rows_send(3)
    raw(RIGHT, 2)
    add(RIGHT, 0)
    y_step(3, (0, 1))
    raw(RIGHT, 4)
    add(RIGHT, 1)
    y_step(3, (2, 3))
    rows_ready(2)
    raw(LEFT, 0, 1)
    add(LEFT, 2)
    y_ready(3)
    far(5, 6)
    raw(LEFT, 3)
    add(LEFT, 4)
    y_step(4, (0, 1))
    add(RIGHT, 3)
    raw(RIGHT, 6)
    raw(LEFT, 5)
    y_ready(4)
    far(7)
    raw(LEFT, 7)
    raw(RIGHT, 7)
    add(RIGHT, 5)
    add(LEFT, 6)
    rows_ready(3)
    for g in range(8):
        hold[at_y(OFFSETS[g])] = piece(3, g)

    for g in range(8):
        where = at_y(OFFSETS[g])
        v = hold[where] + x_take(RIGHT, g) + x_take(LEFT, g)
        hold[where] = v + x_take(FAR, g) if g == STRAIGHT else v

    mine_pair = lax.div(x, 2)

    def block(to_h, i, c):
        pair = to_h * 2 + (1 - mine_pair if i == 0 else mine_pair)
        return hold[2 * lax.div(assign[0, 2 * pair], 2) + c]

    UNITS = [(i, c) for i in range(2) for c in range(2)]
    for i, c in UNITS:
        code, step = encode(block(1 - h, i, c))
        zcs[i, c] = code
        zss[i, c] = step
        start(zcs.at[i, c], zcr.at[i, c], zs.at[0, i, c], zr.at[0, i, c], z_dev)
        start(zss.at[i, c], zsr.at[i, c], zs.at[1, i, c], zr.at[1, i, c], z_dev)

    near = 1 - 2 * lax.rem(x, 2)
    across = [(0, near, 1), (1, 2, 0), (2, -near, 0)]

    def place(where, c, value):
        for q in range(4):
            grad_full[q, where, :, c * HALF:(c + 1) * HALF] = value[q * SUB:(q + 1) * SUB]

    for i, c in UNITS:
        landed(zcr.at[i, c], zs.at[0, i, c], zr.at[0, i, c], z_dev)
        landed(zsr.at[i, c], zs.at[1, i, c], zr.at[1, i, c], z_dev)
        v = block(h, i, c) + decode(zcr[i, c], zsr[i, c])
        code, step = encode(v)
        acs[i, c] = code
        ass_[i, c] = step
        for n, d, unit in across:
            if unit == i:
                start(acs.at[i, c], acr.at[n, c], as_.at[0, n, c], ar.at[0, n, c], x_dev(d))
                start(ass_.at[i, c], asr.at[n, c], as_.at[1, n, c], ar.at[1, n, c], x_dev(d))
        if i == 1:
            place(x, c, v)
    for n, d, unit in (across[1], across[2], across[0]):
        for c in range(2):
            landed(acr.at[n, c], as_.at[0, n, c], ar.at[0, n, c], x_dev(d))
            landed(asr.at[n, c], as_.at[1, n, c], ar.at[1, n, c], x_dev(d))
            place(lax.rem(x + d + X, X), c, decode(acr[n, c], asr[n, c]))

    side_bit = lax.rem(assign[0, t], 2)
    g = grad_full[...].reshape(BS, BS)
    v = split(jnp.where(side_bit == 0, g, g.T))
    ori[0] = v[0]
    ori[1] = v[1]
    stat_in.wait()

    def eye(low_row, count):
        r = lax.broadcasted_iota(jnp.int32, (count, BS), 0) + low_row
        c = lax.broadcasted_iota(jnp.int32, (count, BS), 1)
        return r == c

    def both(ref):
        return ref[0], ref[1]

    def chunk(ref, q):
        return ref[0, pl.ds(q * HALF, HALF)], ref[1, pl.ds(q * HALF, HALF)]

    def put(ref, q, value):
        value = split(value)
        ref[0, pl.ds(q * HALF, HALF)] = value[0]
        ref[1, pl.ds(q * HALF, HALF)] = value[1]

    def update(value, q):
        return (jnp.where(eye(q * HALF, HALF), 5.0, 0.0) - value) * 0.25

    tokens = float(TOK * X * Z_HI)
    for q in range(2):
        square = mm3(chunk(ori, q), both(ori), dot_nt) * (1.0 / tokens)
        damp = jnp.where(eye(q * HALF, HALF), DAMPING, 0.0)
        put(tmp, q, BETA * stat[pl.ds(q * HALF, HALF)] + (1.0 - BETA) * square + damp)
    for q in range(2):
        v = mm3(chunk(r4, q), both(tmp))
        put(mat, q, v)
        put(upd, q, update(v, q))
    for q in range(2):
        put(upd2, q, mm3(chunk(upd, q), both(upd)))
    for q in range(2):
        put(cur, q, mm3(chunk(mine, q), both(upd)))
    for q in range(2):
        put(tmp, q, mm3(chunk(upd2, q), both(upd2)))
    for q in range(2):
        put(upd, q, update(mm3(chunk(tmp, q), both(mat)), q))
    for q in (1, 0):
        v = mm3(chunk(cur, q), both(upd))
        for i in range(2):
            u = 2 * q + i
            value = v[i * UNIT:(i + 1) * UNIT]
            on = eye(u * UNIT, UNIT)
            code, step = encode(jnp.where(on, 0.0, value))
            rcs[u] = code
            rss[u, 0:1] = step
            rss[u, 1:2] = jnp.sum(jnp.where(on, value, 0.0), axis=0, keepdims=True)
            start(rcs.at[u], rcr.at[u], rs.at[0, u], rr.at[0, u], pair_dev)
            start(rss.at[u], rsr.at[u], rs.at[1, u], rr.at[1, u], pair_dev)
        roots_out[pl.ds(q * HALF, HALF)] = v
        put(mine, q, v)
    v = split(grad_full[...].reshape(BS, BS))
    ori[0] = v[0]
    ori[1] = v[1]

    def arrived(u):
        landed(rcr.at[u], rs.at[0, u], rr.at[0, u], pair_dev)
        landed(rsr.at[u], rs.at[1, u], rr.at[1, u], pair_dev)
        value = decode(rcr[u], rsr[u, 0:1]) + jnp.where(eye(u * UNIT, UNIT), rsr[u, 1:2], 0.0)
        value = split(value)
        other[0, pl.ds(u * UNIT, UNIT)] = value[0]
        other[1, pl.ds(u * UNIT, UNIT)] = value[1]

    arrived(2)
    arrived(3)
    half = tuple(
        jnp.where(side_bit == 0, a, b) for a, b in zip(chunk(mine, 0), chunk(other, 1))
    )
    v = split(mm3(half, both(ori)))
    pre[0] = v[0]
    pre[1] = v[1]
    arrived(0)
    arrived(1)
    right = tuple(jnp.where(side_bit == 0, b, a) for a, b in zip(both(mine), both(other)))
    precond_out[...] = mm3(both(pre), right)
    for copy in sends:
        copy.wait_send()


def shards(grad_out, acts, stat_old, root_old, assign):
    def wide(*shape):
        return pltpu.VMEM((*shape, UNIT, BS), jnp.int16)

    def narrow(*shape):
        return pltpu.VMEM((*shape, UNIT, HALF), jnp.int16)

    def steps(count, *shape):
        return pltpu.VMEM((*shape, 1, count), F32)

    def pair_of(rows_):
        return pltpu.VMEM((2, rows_, BS), BF)

    dma = pltpu.SemaphoreType.DMA
    anywhere = pl.BlockSpec(memory_space=pl.ANY)
    vmem = pl.BlockSpec(memory_space=pltpu.VMEM)
    roots, precond = pl.pallas_call(
        kernel,
        out_shape=(
            pltpu.VMEM((BS, BS), F32),
            pltpu.VMEM((HALF, BS), F32),
        ),
        in_specs=[pl.BlockSpec(memory_space=pltpu.SMEM), vmem, vmem, anywhere, anywhere],
        out_specs=(vmem, vmem),
        scratch_shapes=[
            pltpu.VMEM((CORES * Y, TOK, SHARD), BF),
            pltpu.VMEM((X, Z_LO, SUB, TOK), BF),
            pltpu.VMEM((BS, BS), F32),
            pltpu.VMEM((BS, BS), F32),
            pltpu.VMEM((Y, UNIT, HALF), F32),
            pltpu.VMEM((Z_LO, X, SUB, BS), F32),
            *[pair_of(BS) for _ in range(10)],
            pair_of(HALF),
            narrow(3, Y), narrow(3, Y), steps(HALF, 3, Y), steps(HALF, 3, Y),
            narrow(2, 2), narrow(2, 2), steps(HALF, 2, 2), steps(HALF, 2, 2),
            narrow(2, 2), narrow(3, 2), steps(HALF, 2, 2), steps(HALF, 3, 2),
            wide(4), wide(4),
            pltpu.VMEM((4, 2, BS), F32), pltpu.VMEM((4, 2, BS), F32),
            dma((3,)),
            dma((2, 4, 4)), dma((2, 4, 4)),
            dma((29,)), dma((29,)),
            dma((4, 3)), dma((4, 3)),
            dma((2, 3, Y)), dma((2, 3, Y)),
            dma((2, 2, 2)), dma((2, 2, 2)),
            dma((2, 3, 2)), dma((2, 3, 2)),
            dma((2, 4)), dma((2, 4)),
        ],
        compiler_params=pltpu.CompilerParams(
            collective_id=0, has_side_effects=True, vmem_limit_bytes=56 * 2**20
        ),
    )(assign, grad_out, acts, stat_old[0, 0], root_old[0, 0])
    return roots[None, None], precond[None, None]


def solution(mesh):
    placed = (
        P("tok", "blk"),
        P("tok", "blk"),
        P("tok", "blk", None, None),
        P("tok", "blk", None, None),
        P("blk", None),
    )
    return jax.shard_map(
        shards,
        mesh=mesh,
        in_specs=placed,
        out_specs=(P("tok", "blk", None, None), P("tok", "blk", None, None)),
        check_vma=False,
    )
```

time: 96.6 us -> 89.7 us (0.929)
  the two profiles are of different devices: /device:TPU:152 before, /device:TPU:134 now
where the time goes in v2:
time: 89.7 us; the launch traced here: 89.5 us
  Pallas kernels  87.1 us (97%)
  local copies, waits for them, and re-layouts  1.77 us (2%)
    pallas_call x1, Pallas kernels, shards(): pl.pallas_call(kernel, out_shape=(pltpu.VMEM((BS, BS), F32), pltpu.VMEM((...  87.1 us

profile of v2, /device:TPU:134, one launch (start us, length us, event | category | flops | bytes accessed | tf_op | source)
XLA Modules:
  0.0 89.5 jit_solution(7852861582333649731)
XLA Ops:
  0.6 87.1 %shard_map.68 = (f32[512,512]{1,0:T(8,128)S(1)}, f32[256,512]{1,0:T(8,128)S(1)}) custom-call(s32[1,8]{1,0:T(1,128)} %assign.1, bf16[1024,128]{1,0:T(8,128)(2,1)} %grad.1, bf16[1024,128]{1,0:T(8,128)(2,1)} %acts.1, f32[512,512]{1,0:T(8,128)} %bitcast.6, f32[512,512]{1,0:T(8,128)} %bitcast.7), custom_call_target="tpu_custom_call" | custom-call | tf_op jit(solution)/shard_map/pallas_call | solution.py:409
  87.8 1.0 %copy.9 = f32[1,1,512,512]{3,2,1,0:T(8,128)} copy(f32[1,1,512,512]{3,2,1,0:T(8,128)S(1)} %bitcast.4) | data formatting | bytes 2097152
  88.7 0.8 copy.10

commit v3 on v2

--- a/solution.py
+++ b/solution.py
@@ -58,6 +58,7 @@
 def kernel(
     assign, grad, acts, stat_hbm, root_hbm, roots_out, precond_out,
     cols, rows, stat, root, hold, grad_full, ori, r2, r4, mat, upd, cur, upd2, tmp, mine, other, pre,
+    ori_b, r4_b, mat_b, upd_b, cur_b, upd2_b, tmp_b, old_b, stat_b,
     xcs, xcr, xss, xsr, zcs, zcr, zss, zsr, acs, acr, ass_, asr, rcs, rcr, rss, rsr,
     loc_sem, ys, yr, sibs, sibr, ws, wr, xs, xr, zs, zr, as_, ar, rs, rr,
 ):
@@ -167,7 +168,31 @@
             start(unit, unit, ws.at[e, d - 1], wr.at[e, d - 1], w_dev(d))
 
     rows_send(0)
+    def eye(low_row, count):
+        r = lax.broadcasted_iota(jnp.int32, (count, BS), 0) + low_row
+        c = lax.broadcasted_iota(jnp.int32, (count, BS), 1)
+        return r == c
+
+    def old_send(n, ref):
+        for u in range(4):
+            value = ref[pl.ds(u * UNIT, UNIT)]
+            on = eye(u * UNIT, UNIT)
+            code, step = encode(jnp.where(on, 0.0, value))
+            rcs[n, u] = code
+            rss[n, u, 0:1] = step
+            rss[n, u, 1:2] = jnp.sum(jnp.where(on, value, 0.0), axis=0, keepdims=True)
+        start(rcs.at[n], rcr.at[n], rs.at[0, n], rr.at[0, n], pair_dev)
+        start(rss.at[n], rsr.at[n], rs.at[1, n], rr.at[1, n], pair_dev)
+
+    def old_landed(n):
+        landed(rcr.at[n], rs.at[0, n], rr.at[0, n], pair_dev)
+        landed(rsr.at[n], rs.at[1, n], rr.at[1, n], pair_dev)
+
+    def old_take(n, u):
+        return decode(rcr[n, u], rsr[n, u, 0:1]) + jnp.where(eye(u * UNIT, UNIT), rsr[n, u, 1:2], 0.0)
+
     root_in.wait()
+    old_send(0, root)
     x0 = split(root[...])
     mine[0] = x0[0]
     mine[1] = x0[1]
@@ -250,12 +275,14 @@
     add(RIGHT, 3)
     raw(RIGHT, 6)
     raw(LEFT, 5)
+    add(RIGHT, 5)
+    add(LEFT, 6)
     y_ready(4)
     far(7)
     raw(LEFT, 7)
     raw(RIGHT, 7)
-    add(RIGHT, 5)
-    add(LEFT, 6)
+    stat_in.wait()
+    old_send(1, stat)
     rows_ready(3)
     for g in range(8):
         hold[at_y(OFFSETS[g])] = piece(3, g)
@@ -278,6 +305,17 @@
         zss[i, c] = step
         start(zcs.at[i, c], zcr.at[i, c], zs.at[0, i, c], zr.at[0, i, c], z_dev)
         start(zss.at[i, c], zsr.at[i, c], zs.at[1, i, c], zr.at[1, i, c], z_dev)
+
+    old_landed(0)
+    for u in range(4):
+        v = split(old_take(0, u))
+        old_b[0, pl.ds(u * UNIT, UNIT)] = v[0]
+        old_b[1, pl.ds(u * UNIT, UNIT)] = v[1]
+    v = (old_b[0], old_b[1])
+    v = split(mm3(v, v))
+    v = split(mm3(v, v))
+    r4_b[0] = v[0]
+    r4_b[1] = v[1]
 
     near = 1 - 2 * lax.rem(x, 2)
     across = [(0, near, 1), (1, 2, 0), (2, -near, 0)]
@@ -299,6 +337,9 @@
                 start(ass_.at[i, c], asr.at[n, c], as_.at[1, n, c], ar.at[1, n, c], x_dev(d))
         if i == 1:
             place(x, c, v)
+    old_landed(1)
+    for u in range(4):
+        stat_b[pl.ds(u * UNIT, UNIT)] = old_take(1, u)
     for n, d, unit in (across[1], across[2], across[0]):
         for c in range(2):
             landed(acr.at[n, c], as_.at[0, n, c], ar.at[0, n, c], x_dev(d))
@@ -307,15 +348,11 @@
 
     side_bit = lax.rem(assign[0, t], 2)
     g = grad_full[...].reshape(BS, BS)
-    v = split(jnp.where(side_bit == 0, g, g.T))
-    ori[0] = v[0]
-    ori[1] = v[1]
-    stat_in.wait()
-
-    def eye(low_row, count):
-        r = lax.broadcasted_iota(jnp.int32, (count, BS), 0) + low_row
-        c = lax.broadcasted_iota(jnp.int32, (count, BS), 1)
-        return r == c
+    gt = g.T
+    for ref, value in ((ori, jnp.where(side_bit == 0, g, gt)), (ori_b, jnp.where(side_bit == 0, gt, g))):
+        v = split(value)
+        ref[0] = v[0]
+        ref[1] = v[1]
 
     def both(ref):
         return ref[0], ref[1]
@@ -332,60 +369,43 @@
         return (jnp.where(eye(q * HALF, HALF), 5.0, 0.0) - value) * 0.25
 
     tokens = float(TOK * X * Z_HI)
-    for q in range(2):
-        square = mm3(chunk(ori, q), both(ori), dot_nt) * (1.0 / tokens)
-        damp = jnp.where(eye(q * HALF, HALF), DAMPING, 0.0)
-        put(tmp, q, BETA * stat[pl.ds(q * HALF, HALF)] + (1.0 - BETA) * square + damp)
-    for q in range(2):
-        v = mm3(chunk(r4, q), both(tmp))
-        put(mat, q, v)
-        put(upd, q, update(v, q))
-    for q in range(2):
-        put(upd2, q, mm3(chunk(upd, q), both(upd)))
-    for q in range(2):
-        put(cur, q, mm3(chunk(mine, q), both(upd)))
-    for q in range(2):
-        put(tmp, q, mm3(chunk(upd2, q), both(upd2)))
-    for q in range(2):
-        put(upd, q, update(mm3(chunk(tmp, q), both(mat)), q))
-    for q in (1, 0):
+    own_set = (ori, r4, mat, upd, cur, upd2, tmp, mine, stat)
+    other_set = (ori_b, r4_b, mat_b, upd_b, cur_b, upd2_b, tmp_b, old_b, stat_b)
+    sets = (own_set, other_set)
+    halves = range(2)
+    for ori_, r4_, mat_, upd_, cur_, upd2_, tmp_, old_, stat_ in sets:
+        for q in halves:
+            square = mm3(chunk(ori_, q), both(ori_), dot_nt) * (1.0 / tokens)
+            damp = jnp.where(eye(q * HALF, HALF), DAMPING, 0.0)
+            put(tmp_, q, BETA * stat_[pl.ds(q * HALF, HALF)] + (1.0 - BETA) * square + damp)
+    for ori_, r4_, mat_, upd_, cur_, upd2_, tmp_, old_, stat_ in sets:
+        for q in halves:
+            v = mm3(chunk(r4_, q), both(tmp_))
+            put(mat_, q, v)
+            put(upd_, q, update(v, q))
+    for ori_, r4_, mat_, upd_, cur_, upd2_, tmp_, old_, stat_ in sets:
+        for q in halves:
+            put(upd2_, q, mm3(chunk(upd_, q), both(upd_)))
+        for q in halves:
+            put(cur_, q, mm3(chunk(old_, q), both(upd_)))
+    for ori_, r4_, mat_, upd_, cur_, upd2_, tmp_, old_, stat_ in sets:
+        for q in halves:
+            put(tmp_, q, mm3(chunk(upd2_, q), both(upd2_)))
+    for ori_, r4_, mat_, upd_, cur_, upd2_, tmp_, old_, stat_ in sets:
+        for q in halves:
+            put(upd_, q, update(mm3(chunk(tmp_, q), both(mat_)), q))
+    for q in halves:
         v = mm3(chunk(cur, q), both(upd))
-        for i in range(2):
-            u = 2 * q + i
-            value = v[i * UNIT:(i + 1) * UNIT]
-            on = eye(u * UNIT, UNIT)
-            code, step = encode(jnp.where(on, 0.0, value))
-            rcs[u] = code
-            rss[u, 0:1] = step
-            rss[u, 1:2] = jnp.sum(jnp.where(on, value, 0.0), axis=0, keepdims=True)
-            start(rcs.at[u], rcr.at[u], rs.at[0, u], rr.at[0, u], pair_dev)
-            start(rss.at[u], rsr.at[u], rs.at[1, u], rr.at[1, u], pair_dev)
         roots_out[pl.ds(q * HALF, HALF)] = v
         put(mine, q, v)
+        put(other, q, mm3(chunk(cur_b, q), both(upd_b)))
     v = split(grad_full[...].reshape(BS, BS))
-    ori[0] = v[0]
-    ori[1] = v[1]
-
-    def arrived(u):
-        landed(rcr.at[u], rs.at[0, u], rr.at[0, u], pair_dev)
-        landed(rsr.at[u], rs.at[1, u], rr.at[1, u], pair_dev)
-        value = decode(rcr[u], rsr[u, 0:1]) + jnp.where(eye(u * UNIT, UNIT), rsr[u, 1:2], 0.0)
-        value = split(value)
-        other[0, pl.ds(u * UNIT, UNIT)] = value[0]
-        other[1, pl.ds(u * UNIT, UNIT)] = value[1]
-
-    arrived(2)
-    arrived(3)
     half = tuple(
         jnp.where(side_bit == 0, a, b) for a, b in zip(chunk(mine, 0), chunk(other, 1))
     )
-    v = split(mm3(half, both(ori)))
-    pre[0] = v[0]
-    pre[1] = v[1]
-    arrived(0)
-    arrived(1)
+    v = split(mm3(half, v))
     right = tuple(jnp.where(side_bit == 0, b, a) for a, b in zip(both(mine), both(other)))
-    precond_out[...] = mm3(both(pre), right)
+    precond_out[...] = mm3(v, right)
     for copy in sends:
         copy.wait_send()
 
@@ -423,11 +443,13 @@
             pltpu.VMEM((Z_LO, X, SUB, BS), F32),
             *[pair_of(BS) for _ in range(10)],
             pair_of(HALF),
+            *[pair_of(BS) for _ in range(8)],
+            pltpu.VMEM((BS, BS), F32),
             narrow(3, Y), narrow(3, Y), steps(HALF, 3, Y), steps(HALF, 3, Y),
             narrow(2, 2), narrow(2, 2), steps(HALF, 2, 2), steps(HALF, 2, 2),
             narrow(2, 2), narrow(3, 2), steps(HALF, 2, 2), steps(HALF, 3, 2),
-            wide(4), wide(4),
-            pltpu.VMEM((4, 2, BS), F32), pltpu.VMEM((4, 2, BS), F32),
+            wide(2, 4), wide(2, 4),
+            pltpu.VMEM((2, 4, 2, BS), F32), pltpu.VMEM((2, 4, 2, BS), F32),
             dma((3,)),
             dma((2, 4, 4)), dma((2, 4, 4)),
             dma((29,)), dma((29,)),
@@ -435,7 +457,7 @@
             dma((2, 3, Y)), dma((2, 3, Y)),
             dma((2, 2, 2)), dma((2, 2, 2)),
             dma((2, 3, 2)), dma((2, 3, 2)),
-            dma((2, 4)), dma((2, 4)),
+            dma((2, 2)), dma((2, 2)),
         ],
         compiler_params=pltpu.CompilerParams(
             collective_id=0, has_side_effects=True, vmem_limit_bytes=56 * 2**20

time: 89.7 us -> 85.1 us (0.949)
  the two profiles are of different devices: /device:TPU:134 before, /device:TPU:16 now
where the time goes in v3:
time: 85.1 us; the launch traced here: 85 us
  Pallas kernels  82.6 us (97%)
  local copies, waits for them, and re-layouts  1.77 us (2%)
    pallas_call x1, Pallas kernels, shards(): pl.pallas_call(kernel, out_shape=(pltpu.VMEM((BS, BS), F32), pltpu.VMEM((...  82.6 us
    unnamed x2, local copies, waits for them, and re-layouts  1.77 us

profile of v3, /device:TPU:16, one launch (start us, length us, event | category | flops | bytes accessed | tf_op | source)
XLA Modules:
  0.0 85.0 jit_solution(9658120358185532138)
XLA Ops:
  0.6 82.6 %shard_map.68 = (f32[512,512]{1,0:T(8,128)S(1)}, f32[256,512]{1,0:T(8,128)S(1)}) custom-call(s32[1,8]{1,0:T(1,128)} %assign.1, bf16[1024,128]{1,0:T(8,128)(2,1)} %grad.1, bf16[1024,128]{1,0:T(8,128)(2,1)} %acts.1, f32[512,512]{1,0:T(8,128)} %bitcast.6, f32[512,512]{1,0:T(8,128)} %bitcast.7), custom_call_target="tpu_custom_call" | custom-call | tf_op jit(solution)/shard_map/pallas_call | solution.py:429
  83.2 1.0 %copy.9 = f32[1,1,512,512]{3,2,1,0:T(8,128)} copy(f32[1,1,512,512]{3,2,1,0:T(8,128)S(1)} %bitcast.4) | data formatting | bytes 2097152
  84.2 0.8 copy.10

commit v4 on v3

--- a/solution.py
+++ b/solution.py
@@ -196,12 +196,6 @@
     x0 = split(root[...])
     mine[0] = x0[0]
     mine[1] = x0[1]
-    v = split(mm3(x0, x0))
-    r2[0] = v[0]
-    r2[1] = v[1]
-    v = split(mm3(v, v))
-    r4[0] = v[0]
-    r4[1] = v[1]
 
     scaling = 1.0 / math.sqrt(TOK * X * Z_HI)
 
@@ -317,6 +311,13 @@
     r4_b[0] = v[0]
     r4_b[1] = v[1]
 
+    v = split(mm3((mine[0], mine[1]), (mine[0], mine[1])))
+    r2[0] = v[0]
+    r2[1] = v[1]
+    v = split(mm3(v, v))
+    r4[0] = v[0]
+    r4[1] = v[1]
+
     near = 1 - 2 * lax.rem(x, 2)
     across = [(0, near, 1), (1, 2, 0), (2, -near, 0)]
 

time: 85.1 us -> 85.2 us (level)
  no operation moved by 1% of the time
where the time goes in v4:
time: 85.2 us; the launch traced here: 85 us
  Pallas kernels  82.6 us (97%)
  local copies, waits for them, and re-layouts  1.77 us (2%)
    pallas_call x1, Pallas kernels, shards(): pl.pallas_call(kernel, out_shape=(pltpu.VMEM((BS, BS), F32), pltpu.VMEM((...  82.6 us
    unnamed x2, local copies, waits for them, and re-layouts  1.77 us

profile of v4, /device:TPU:16, one launch (start us, length us, event | category | flops | bytes accessed | tf_op | source)
XLA Modules:
  0.0 85.0 jit_solution(2663264445721686877)
XLA Ops:
  0.6 82.6 %shard_map.68 = (f32[512,512]{1,0:T(8,128)S(1)}, f32[256,512]{1,0:T(8,128)S(1)}) custom-call(s32[1,8]{1,0:T(1,128)} %assign.1, bf16[1024,128]{1,0:T(8,128)(2,1)} %grad.1, bf16[1024,128]{1,0:T(8,128)(2,1)} %acts.1, f32[512,512]{1,0:T(8,128)} %bitcast.6, f32[512,512]{1,0:T(8,128)} %bitcast.7), custom_call_target="tpu_custom_call" | custom-call | tf_op jit(solution)/shard_map/pallas_call | solution.py:430
  83.3 1.0 %copy.9 = f32[1,1,512,512]{3,2,1,0:T(8,128)} copy(f32[1,1,512,512]{3,2,1,0:T(8,128)S(1)} %bitcast.4) | data formatting | bytes 2097152
  84.2 0.8 copy.10
